TPU v7x, 128 devices: a whole 4x4x4 slice. The times are simulated.
128 devices in a mesh: dp: 4 (over x), section: 4 (over y_hi, core), expert: 8 (over y_lo, z).
Axes of the slice: x: 4, y: 4 (y_hi: 2, y_lo: 2; y = y_hi * 2 + y_lo), z: 4, core: 2. Of those that a mesh axis runs over, the one named last changes fastest.
Arguments:
- tokens: bfloat16 [8192, 4096], P(('dp', 'section')), may hold values from -90 to 90
- w_query: bfloat16 [4096, 2048], P(None, 'expert'), may hold values from -0.09375 to 0.09375
- w_key: bfloat16 [4096, 1024], P(None, 'expert'), may hold values from -0.09375 to 0.09375
- w_value: bfloat16 [4096, 1024], P(None, 'expert'), may hold values from -0.09375 to 0.09375
- w_out: bfloat16 [2048, 4096], P('expert'), may hold values from -0.125 to 0.125
- w_gate: bfloat16 [8, 7168, 4096], P('expert', ('dp', 'section')), may hold values from -0.09375 to 0.09375
- w_up: bfloat16 [8, 7168, 4096], P('expert', ('dp', 'section')), may hold values from -0.09375 to 0.09375
- w_down: bfloat16 [8, 7168, 4096], P('expert', ('dp', 'section')), may hold values from -0.0625 to 0.0625
- route: int32 [128, 1], P(('dp', 'section')), may hold values from 0 to 7; in each aligned block of 8 rows (0 to 7, 8 to 15, ...) at most 2 rows name the same one
- old_out: bfloat16 [128, 64, 4096], P(('dp', 'section'), 'expert'), may hold values from -6 to 6
- cotangent: bfloat16 [8192, 4096], P(('dp', 'section')), may hold values from -6 to 6
Outputs:
- joined: bfloat16 [128, 64, 4096], P(('dp', 'section'), 'expert')
- divergence: float32 [128, 64], P(('dp', 'section'), 'expert')
- grad_out_t: float32 [4096, 2048], P(('dp', 'section'), 'expert')
Inputs may be any that keep to these rules, and one draw needn't show every extreme that they name: `route`: blocks routed to experts 6 and above go to new experts. Among the 8 blocks of one replica no expert is named more than 2 times, and some replica names one expert exactly 2 times in every draw.
All inputs are finite; a program needn't handle non-finite values.
Results may differ from a plain program's by a relative error of at most 0.025.
Values may be sent and summed in bfloat16 or wider, within the bound.
No kernel may reach another device: no remote copies, remote signals or barrier semaphores. Data moves between devices by JAX's collectives and lax.ppermute only.
A program may use at most 192 MiB of HBM per device.

v0:
```python
import math
import jax
import jax.numpy as jnp
from jax import lax
from jax.sharding import PartitionSpec as P

D = 4096
HEAD_DIM = 128
BLOCK = 64


def in_blocks(value, dim, length):
    shape = value.shape
    parts = value.reshape(*shape[:dim], length, shape[dim] // length, *shape[dim + 1 :])
    return jnp.moveaxis(parts, dim, 0)


def sum_at_owner(value, axis, dim):
    parts = in_blocks(value, dim, lax.axis_size(axis))
    arrived = lax.all_to_all(parts, axis, split_axis=0, concat_axis=0, tiled=True)
    return arrived.astype(jnp.float32).sum(axis=0)


def attend_local(tokens, w_query, w_key, w_value):
    length = tokens.shape[0]
    key_heads = w_key.shape[1] // HEAD_DIM
    group = w_query.shape[1] // w_key.shape[1]
    queries = jnp.dot(tokens, w_query, preferred_element_type=jnp.float32).astype(jnp.bfloat16)
    queries = queries.reshape(length, key_heads, group, HEAD_DIM)
    keys = jnp.dot(tokens, w_key, preferred_element_type=jnp.float32).astype(jnp.bfloat16)
    keys = keys.reshape(length, key_heads, HEAD_DIM)
    values = jnp.dot(tokens, w_value, preferred_element_type=jnp.float32).astype(jnp.bfloat16)
    values = values.reshape(length, key_heads, HEAD_DIM)
    height = min(length, 512)

    def one_block(number):
        first = number * height
        scores = jnp.einsum("qkgd,skd->kgqs", queries, keys, preferred_element_type=jnp.float32)
        scores = scores * (1.0 / math.sqrt(HEAD_DIM))
        query_pos = first + lax.broadcasted_iota(jnp.int32, (height, length), 0)
        key_pos = lax.broadcasted_iota(jnp.int32, (height, length), 1)
        scores = jnp.where(query_pos >= key_pos, scores, -jnp.inf)
        top = jnp.max(scores, axis=-1, keepdims=True)
        weights = jnp.exp(scores - top)
        probs = (weights / jnp.sum(weights, axis=-1, keepdims=True)).astype(jnp.bfloat16)
        mixed = jnp.einsum("kgqs,skd->qkgd", probs, values, preferred_element_type=jnp.float32)
        return mixed.astype(jnp.bfloat16)

    mixed = lax.map(one_block, jnp.arange(length // height, dtype=jnp.int32))
    return mixed.reshape(length, key_heads * group * HEAD_DIM)


def routing_table(routes, experts, capacity):
    number = routes.shape[0]
    same = routes[:, None] == routes[None, :]
    earlier = lax.broadcasted_iota(jnp.int32, (number, number), 1) < lax.broadcasted_iota(
        jnp.int32, (number, number), 0
    )
    slot = jnp.sum((same & earlier).astype(jnp.int32), axis=1)
    expert_hit = routes[None, :] == lax.broadcasted_iota(jnp.int32, (experts, number), 0)
    slot_hit = slot[None, :] == lax.broadcasted_iota(jnp.int32, (capacity, number), 0)
    return (expert_hit[:, None, :] & slot_hit[None, :, :]).astype(jnp.bfloat16)


def wo_gradient(cotangent, heads_out):
    return sum_at_owner(
        lax.dot_general(
            cotangent, heads_out, (((0,), (0,)), ((), ())), preferred_element_type=jnp.float32
        ).astype(jnp.bfloat16),
        ("dp", "section"),
        0,
    )


def per_device(
    tokens, w_query, w_key, w_value, w_out, w_gate, w_up, w_down, route, old_out, cotangent
):
    experts = lax.axis_size("expert")
    own_index = lax.axis_index("expert")
    length = tokens.shape[0]
    blocks = length // BLOCK
    piece_rows = BLOCK // experts
    capacity = max(2, blocks // experts + 1)
    old_count = experts - max(1, experts // 4)
    routes = route[:, 0]
    table = routing_table(routes, experts, capacity)
    heads_out = attend_local(tokens, w_query, w_key, w_value)
    partial_value = jnp.dot(heads_out, w_out, preferred_element_type=jnp.float32).reshape(
        blocks, BLOCK, D
    )
    token_blocks = tokens.reshape(blocks, BLOCK, D)
    attention = lax.psum_scatter(
        partial_value.astype(jnp.bfloat16), "expert", scatter_dimension=1, tiled=True
    ).astype(jnp.float32)
    own_rows = lax.dynamic_slice_in_dim(token_blocks, own_index * piece_rows, piece_rows, 1)
    hidden_in = (own_rows.astype(jnp.float32) + attention).astype(jnp.bfloat16)
    outgoing = jnp.einsum(
        "jcb,brd->jcrd", table, hidden_in, preferred_element_type=jnp.float32
    ).astype(jnp.bfloat16)
    arrived = lax.all_to_all(outgoing, "expert", split_axis=0, concat_axis=0, tiled=True)
    expert_rows = arrived.reshape(experts * capacity * piece_rows, D)
    gate_rows = w_gate[0]
    up_rows = w_up[0]
    down_rows = w_down[0]
    contract = (((1,), (1,)), ((), ()))
    piece = lax.all_gather(expert_rows, ("dp", "section"), axis=0, tiled=True)
    gate = lax.dot_general(piece, gate_rows, contract, preferred_element_type=jnp.float32)
    lifted = lax.dot_general(piece, up_rows, contract, preferred_element_type=jnp.float32)
    active = (jax.nn.silu(gate) * lifted).astype(jnp.bfloat16)
    expert_sum = lax.psum_scatter(
        jnp.dot(active, down_rows, preferred_element_type=jnp.float32).astype(jnp.bfloat16),
        ("dp", "section"),
        scatter_dimension=0,
        tiled=True,
    )
    returned = lax.all_to_all(
        expert_sum.reshape(experts, capacity, piece_rows, D),
        "expert",
        split_axis=0,
        concat_axis=0,
        tiled=True,
    )
    merged = jnp.einsum("jcb,jcrd->brd", table, returned, preferred_element_type=jnp.float32)
    joined = (hidden_in.astype(jnp.float32) + merged).astype(jnp.bfloat16)
    fresh = (routes >= old_count).astype(jnp.float32)
    gap = joined.astype(jnp.float32) - old_out.astype(jnp.float32)
    divergence = 0.5 * jnp.mean(gap * gap, axis=-1) * fresh[:, None]
    gradient = wo_gradient(cotangent, heads_out)
    return (joined, divergence, gradient)


def solution(mesh):
    return jax.shard_map(
        per_device,
        mesh=mesh,
        in_specs=(
            P(("dp", "section"), None),
            P(None, "expert"),
            P(None, "expert"),
            P(None, "expert"),
            P("expert", None),
            P("expert", ("dp", "section"), None),
            P("expert", ("dp", "section"), None),
            P("expert", ("dp", "section"), None),
            P(("dp", "section"), None),
            P(("dp", "section"), "expert", None),
            P(("dp", "section"), None),
        ),
        out_specs=(
            P(("dp", "section"), "expert", None),
            P(("dp", "section"), "expert"),
            P(("dp", "section"), "expert"),
        ),
        check_vma=False,
    )
```

profile of v0, /device:TPU:1, one launch (start us, length us, event | category | flops | bytes accessed | tf_op | source)
XLA Modules:
  0.0 434.4 jit_solution(16842746482815868025)
XLA Ops:
  7.2 0.0 copy-start
  7.2 0.0 reduce-scatter.7.cloned.1.call-start
  7.2 0.1 iota_compare_fusion
  7.3 0.0 copy-start.3
  7.3 5.0 %convolution_convert_fusion.5 = bf16[512,256]{0,1:T(8,128)(2,1)} fusion(bf16[512,4096]{1,0:T(8,128)(2,1)} %param.11, bf16[4096,256]{1,0:T(8,128)(2,1)} %param.12), kind=kOutput, calls=%fused_computation.22 | convolution fusion | flops 1073872896 | bytes 6553600 | tf_op jit(solution)/shard_map/dot_general | solution.py:28
  12.3 0.0 copy-done.3
  12.3 5.6 %fusion.27 = (f32[2,512]{1,0:T(2,128)S(1)}, f32[1,2,512,512]{2,3,1,0:T(8,128)}) fusion(bf16[512,2,128]{0,2,1:T(8,128)(2,1)} %bitcast.121, bf16[512,4096]{1,0:T(8,128)(2,1)} %param.11, bf16[4096,128]{1,0:T(8,128)(2,1)S(1)} %copy-done.3, pred[512,512]{0,1:T(8,128)(4,1)S(1)} %iota_compare_fusion), kind=kOutput, calls=%fused_computation.51 | convolution fusion | flops 672726016 | bytes 7868416 | tf_op jit(solution)/shard_map/while/body/eval_jaxpr/qkgd,skd->kgqs/dot_general | solution.py:38
  18.0 1.9 fusion.12
  19.9 4.9 %convolution_convert_fusion.4 = bf16[128,2,512]{2,0,1:T(8,128)(2,1)S(1)} fusion(bf16[512,4096]{1,0:T(8,128)(2,1)} %param.11, bf16[4096,128]{1,0:T(8,128)(2,1)} %param.14, f32[1,2,512,512]{2,3,1,0:T(8,128)} %get-tuple-element.28, f32[2,512]{1,0:T(2,128)S(1)} %fusion.12, f32[2,512]{1,0:T(2,128)S(1)} %get-tuple-element.27), kind=kOutput, calls=%fused_computation.21 | convolution fusion | flops 672858112 | bytes 7610368 | tf_op jit(solution)/shard_map/while/body/eval_jaxpr/kgqs,skd->qkgd/dot_general | solution.py:46
  24.8 0.2 copy.62
  24.9 0.2 dot_general.45
  25.1 0.0 copy-done
  25.1 1.3 fusion.28
  26.4 2.2 copy.87
  28.6 0.0 copy-start.4
  28.6 0.0 reduce-scatter.7.cloned.1.call-update
  28.6 0.0 all-gather.2.cloned.1.call-start
  28.7 0.6 copy-done.4
  29.3 0.1 convert_reduce_fusion.1
  29.4 0.1 iota_compare_fusion.2
  29.4 1.1 constant_dynamic-slice_fusion
  30.5 54.8 %reduce-scatter.7.cloned.1.call-done = bf16[8,32768]{1,0:T(8,128)(2,1)} async-done(((bf16[64,32768]{1,0:T(8,128)(2,1)}), bf16[8,32768]{1,0:T(8,128)(2,1)}) %reduce-scatter.7.cloned.1.call-update) | async-done | bytes 524304
  85.3 2.3 convolution_convert_fusion.3
  87.7 0.6 copy.65
  88.3 17.5 %all_to_all.15 = bf16[8,2,8,4096]{3,2,1,0:T(8,128)(2,1)} all-to-all(bf16[8,2,8,4096]{3,2,1,0:T(8,128)(2,1)S(1)} %copy.65), channel_id=1, replica_groups=mesh['dp'=4,'section'=4,'expert'=8] {'expert'}, dimensions={0} | all-to-all | bytes 2097152 | tf_op jit(solution)/shard_map/all_to_all | solution.py:100
  105.8 0.0 all-gather.2.cloned.1.call-update
  105.8 0.2 reduce-scatter.5.cloned.1.call-start
  106.0 110.8 %all-gather.2.cloned.1.call-done = bf16[2048,4096]{1,0:T(8,128)(2,1)} async-done(((bf16[128,4096]{1,0:T(8,128)(2,1)}), bf16[2048,4096]{1,0:T(8,128)(2,1)}) %all-gather.2.cloned.1.call-update) | async-done | bytes 16777232 | tf_op jit(solution)/shard_map/all_gather | solution.py:106
  216.8 13.7 %fusion.5 = f32[2048,448]{0,1:T(8,128)} fusion(bf16[2048,4096]{1,0:T(8,128)(2,1)} %all-gather.2.cloned.1.call-done, bf16[1,448,4096]{2,1,0:T(8,128)(2,1)} %param.16), kind=kOutput, calls=%fused_computation.11 | convolution fusion | flops 7516192768 | bytes 24117248 | tf_op jit(solution)/shard_map/dot_general | solution.py:107
  230.5 24.4 %convolution_convert_fusion = bf16[2048,4096]{1,0:T(8,128)(2,1)} fusion(bf16[1,448,4096]{2,1,0:T(8,128)(2,1)} %param.18, f32[2048,448]{0,1:T(8,128)} %fusion.5, bf16[2048,4096]{1,0:T(8,128)(2,1)} %all-gather.2.cloned.1.call-done, bf16[1,448,4096]{2,1,0:T(8,128)(2,1)} %param.17), kind=kOutput, calls=%fused_computation | convolution fusion | flops 15046279168 | bytes 44564480 | tf_op jit(solution)/shard_map/dot_general | solution.py:111
  254.9 0.0 reduce-scatter.5.cloned.1.call-update
  254.9 3.4 convolution_convert_fusion.2
  258.3 1.5 copy.108
  259.9 4.4 %all-to-all-start.2 = ((bf16[16,256,256]{1,2,0:T(8,128)(2,1)}), bf16[16,256,256]{1,2,0:T(8,128)(2,1)}, u32[]{:S(2)}, u32[]{:S(2)}) async-start(bf16[16,256,256]{1,2,0:T(8,128)(2,1)} %bitcast.109), calls=%async_computation.3 | async-start | bytes 4194304 | tf_op jit(solution)/shard_map/all_to_all | solution.py:20
  264.3 0.0 copy-start.2
  264.3 135.2 %reduce-scatter.5.cloned.1.call-done = bf16[128,4096]{1,0:T(8,128)(2,1)} async-done(((bf16[2048,4096]{1,0:T(8,128)(2,1)}), bf16[128,4096]{1,0:T(8,128)(2,1)}) %reduce-scatter.5.cloned.1.call-update) | async-done | bytes 1048592 | tf_op jit(solution)/shard_map/reduce_scatter | solution.py:110
  399.5 3.3 copy.66
  402.8 0.0 all-to-all-done.2
  402.8 4.5 %all-to-all-start.1 = ((bf16[8,2,8,4096]{3,1,2,0:T(2,128)(2,1)}), bf16[8,2,8,4096]{3,1,2,0:T(2,128)(2,1)}, u32[]{:S(2)}, u32[]{:S(2)}) async-start(bf16[8,2,8,4096]{3,1,2,0:T(2,128)(2,1)} %copy.66), calls=%async_computation.2 | async-start | bytes 2097152 | tf_op jit(solution)/shard_map/all_to_all | solution.py:116
  407.2 0.0 copy-start.1
  407.3 2.0 convert_reduce_fusion
  409.3 0.8 copy.73
  410.2 12.2 %all-to-all-done.1 = bf16[8,2,8,4096]{3,1,2,0:T(2,128)(2,1)} async-done(((bf16[8,2,8,4096]{3,1,2,0:T(2,128)(2,1)}), bf16[8,2,8,4096]{3,1,2,0:T(2,128)(2,1)}, u32[]{:S(2)}, u32[]{:S(2)}) %all-to-all-start.1) | async-done | bytes 1048608 | tf_op jit(solution)/shard_map/all_to_all | solution.py:116
  422.3 0.0 copy-done.2
  422.3 3.7 multiply_reduce_fusion
  426.1 1.1 copy.71
  427.2 0.7 copy.72
  427.8 0.0 copy-done.1
  (3 shorter events, 0.0 us)
Async XLA Ops:
  7.2 18.0 %copy-start = (bf16[256,4096]{1,0:T(8,128)(2,1)S(1)}, bf16[256,4096]{1,0:T(8,128)(2,1)}, u32[]{:S(2)}) copy-start(bf16[256,4096]{1,0:T(8,128)(2,1)} %param.15) | copy-start | bytes 6291460
  7.2 78.2 %reduce-scatter.7.cloned.1.call-start = ((), (), s32[]{:S(2)}) async-start(), calls=%async_computation.7 | async-start | bytes 4718592
  7.3 5.0 %copy-start.3 = (bf16[4096,128]{1,0:T(8,128)(2,1)S(1)}, bf16[4096,128]{1,0:T(8,128)(2,1)}, u32[]{:S(2)}) copy-start(bf16[4096,128]{1,0:T(8,128)(2,1)} %param.13) | copy-start | bytes 3145732
  28.6 0.7 copy-start.4
  28.6 188.2 %all-gather.2.cloned.1.call-start = ((), (), s32[]{:S(2)}) async-start(), calls=%async_computation.5 | async-start | bytes 17825792 | tf_op jit(solution)/shard_map/all_gather | solution.py:106
  105.8 293.7 %reduce-scatter.5.cloned.1.call-start = ((), (), s32[]{:S(2)}) async-start(), calls=%async_computation.6 | async-start | bytes 17825792 | tf_op jit(solution)/shard_map/reduce_scatter | solution.py:110
  259.9 142.9 %all-to-all-start.2 = ((bf16[16,256,256]{1,2,0:T(8,128)(2,1)}), bf16[16,256,256]{1,2,0:T(8,128)(2,1)}, u32[]{:S(2)}, u32[]{:S(2)}) async-start(bf16[16,256,256]{1,2,0:T(8,128)(2,1)} %bitcast.109), calls=%async_computation.3 | async-start | bytes 4194304 | tf_op jit(solution)/shard_map/all_to_all | solution.py:20
  264.3 158.1 %copy-start.2 = (bf16[8,32768]{1,0:T(8,128)(2,1)S(1)}, bf16[8,32768]{1,0:T(8,128)(2,1)}, u32[]{:S(2)}) copy-start(bf16[8,32768]{1,0:T(8,128)(2,1)} %reduce-scatter.7.cloned.1.call-done) | copy-start | bytes 1572868
  402.8 19.5 %all-to-all-start.1 = ((bf16[8,2,8,4096]{3,1,2,0:T(2,128)(2,1)}), bf16[8,2,8,4096]{3,1,2,0:T(2,128)(2,1)}, u32[]{:S(2)}, u32[]{:S(2)}) async-start(bf16[8,2,8,4096]{3,1,2,0:T(2,128)(2,1)} %copy.66), calls=%async_computation.2 | async-start | bytes 2097152 | tf_op jit(solution)/shard_map/all_to_all | solution.py:116
  407.2 20.6 %copy-start.1 = (bf16[256,4096]{1,0:T(8,128)(2,1)S(1)}, bf16[256,4096]{1,0:T(8,128)(2,1)}, u32[]{:S(2)}) copy-start(bf16[256,4096]{1,0:T(8,128)(2,1)} %param.15) | copy-start | bytes 6291460
Sparse Core Ops, SparseCore 0:
  28.7 56.5 reduce-scatter.6
  105.9 110.8 all-gather.1
  255.0 144.4 reduce-scatter.4
where the time goes:
time: 435 us; the launch traced here: 434 us
  waiting for transfers between devices  313 us (72%)
  matrix products  64.4 us (15%)
  blocking collectives  17.5 us (4%)
  between operations  13.9 us (3%)
  local copies, waits for them, and re-layouts  12.2 us (3%)
  starting transfers between devices  9.16 us (2%)
    reduce_scatter x1, waiting for transfers between devices, per_device(): lax.psum_scatter(jnp.dot(active, down_rows, preferred_element_type=jnp.fl...  135 us
    all_gather x1, waiting for transfers between devices, per_device(): piece = lax.all_gather(expert_rows, ('dp', 'section'), axis=0, tiled=True)  111 us
    unnamed x4, waiting for transfers between devices  54.9 us
    dot_general x1, matrix products, per_device(): jnp.dot(active, down_rows, preferred_element_type=jnp.float32)  24.4 us
    all_to_all x1, blocking collectives, per_device(): lax.all_to_all(outgoing, 'expert', split_axis=0, concat_axis=0, tiled=True)  17.5 us
    dot_general x1, matrix products, per_device(): lax.dot_general(piece, gate_rows, contract, preferred_element_type=jnp.fl...  13.7 us
    all_to_all x1, waiting for transfers between devices, per_device(): lax.all_to_all(expert_sum.reshape(experts, capacity, piece_rows, D), 'exp...  12.2 us
  transfers between devices with their start and end apart: 5, of which 4 were waited for; matrix products, arithmetic and copies ran while one was open for 3% of the time, Pallas kernels for 0%

commit v1 on v0

--- a/solution.py
+++ b/solution.py
@@ -103,7 +103,12 @@
     up_rows = w_up[0]
     down_rows = w_down[0]
     contract = (((1,), (1,)), ((), ()))
-    piece = lax.all_gather(expert_rows, ("dp", "section"), axis=0, tiled=True)
+    piece = jnp.concatenate(
+        lax.all_to_all(
+            jnp.stack([expert_rows] * lax.axis_size(("dp", "section"))), ("dp", "section"), 0, 0
+        ),
+        axis=0,
+    )
     gate = lax.dot_general(piece, gate_rows, contract, preferred_element_type=jnp.float32)
     lifted = lax.dot_general(piece, up_rows, contract, preferred_element_type=jnp.float32)
     active = (jax.nn.silu(gate) * lifted).astype(jnp.bfloat16)

time: 435 us -> 520 us (1.20)
  blocking collectives: 17.5 us -> 211 us
  waiting for transfers between devices: 313 us -> 200 us
  local copies, waits for them, and re-layouts: 12.2 us -> 19.9 us
    all_to_all x0 -> x1, blocking collectives: none -> 194 us  [per_device(): lax.all_to_all(jnp.stack([expert_rows] * lax.axis_size(('dp', 'section'))...]
    all_gather x1 -> x0, waiting for transfers between devices: 111 us -> none  [per_device(): piece = lax.all_gather(expert_rows, ('dp', 'section'), axis=0, tiled=True)]
    unnamed x14 -> x18, local copies, waits for them, and re-layouts: 5.39 us -> 11.1 us
    unnamed x4 -> x3, waiting for transfers between devices: 54.9 us -> 54.9 us
  transfers between devices with their start and end apart: 5 -> 4, of which waited for: 4 -> 3; matrix products, arithmetic and copies ran while one was open for 3% -> 2% of each run, Pallas kernels for 0% -> 0%
where the time goes in v1:
time: 520 us
  blocking collectives  211 us (41%)
  waiting for transfers between devices  200 us (38%)
  matrix products  60.3 us (12%)
  local copies, waits for them, and re-layouts  19.9 us (4%)
  between operations  14.2 us (3%)
  starting transfers between devices  10.1 us (2%)
    all_to_all x1, blocking collectives, per_device(): lax.all_to_all(jnp.stack([expert_rows] * lax.axis_size(('dp', 'section'))...  194 us
    reduce_scatter x1, waiting for transfers between devices, per_device(): lax.psum_scatter(jnp.dot(active, down_rows, preferred_element_type=jnp.fl...  134 us
    unnamed x3, waiting for transfers between devices  54.9 us
    dot_general x1, matrix products, per_device(): jnp.dot(active, down_rows, preferred_element_type=jnp.float32)  24.4 us
    all_to_all x1, blocking collectives, per_device(): lax.all_to_all(outgoing, 'expert', split_axis=0, concat_axis=0, tiled=True)  16.8 us
    all_to_all x1, waiting for transfers between devices, per_device(): lax.all_to_all(expert_sum.reshape(experts, capacity, piece_rows, D), 'exp...  11.3 us
    unnamed x18, local copies, waits for them, and re-layouts  11.1 us
  transfers between devices with their start and end apart: 4, of which 3 were waited for; matrix products, arithmetic and copies ran while one was open for 2% of the time, Pallas kernels for 0%

profile of v1, /device:TPU:1, one launch (start us, length us, event | category | flops | bytes accessed | tf_op | source)
XLA Modules:
  0.0 519.6 jit_solution(8141521332744974606)
XLA Ops:
  7.2 0.0 copy-start
  7.2 0.0 reduce-scatter.7.cloned.1.call-start
  7.2 0.1 iota_compare_fusion
  7.3 0.0 copy-start.5
  7.3 5.0 convolution_convert_fusion.5
  12.3 0.0 copy-done.5
  12.3 5.6 %fusion.27 = (f32[2,512]{1,0:T(2,128)S(1)}, f32[1,2,512,512]{2,3,1,0:T(8,128)}) fusion(bf16[512,2,128]{0,2,1:T(8,128)(2,1)} %bitcast.124, bf16[512,4096]{1,0:T(8,128)(2,1)} %param.11, bf16[4096,128]{1,0:T(8,128)(2,1)S(1)} %copy-done.5, pred[512,512]{0,1:T(8,128)(4,1)S(1)} %iota_compare_fusion), kind=kOutput, calls=%fused_computation.51 | convolution fusion | flops 672726016 | bytes 7868416 | tf_op jit(solution)/shard_map/while/body/eval_jaxpr/qkgd,skd->kgqs/dot_general | solution.py:38
  18.0 1.9 fusion.12
  19.9 4.9 convolution_convert_fusion.4
  24.8 0.2 copy.62
  24.9 0.2 dot_general.45
  25.1 0.0 copy-done
  25.1 1.3 fusion.28
  26.4 2.2 copy.87
  28.6 0.0 reduce-scatter.7.cloned.1.call-update
  28.6 0.0 reduce-scatter.5.cloned.1.call-start
  28.7 0.6 copy-done.6
  29.3 0.1 convert_reduce_fusion.1
  29.4 0.1 iota_compare_fusion.2
  29.4 1.1 constant_dynamic-slice_fusion
  30.5 54.8 %reduce-scatter.7.cloned.1.call-done = bf16[8,32768]{1,0:T(8,128)(2,1)} async-done(((bf16[64,32768]{1,0:T(8,128)(2,1)}), bf16[8,32768]{1,0:T(8,128)(2,1)}) %reduce-scatter.7.cloned.1.call-update) | async-done | bytes 524304
  85.3 2.3 convolution_convert_fusion.3
  87.7 0.6 copy.65
  88.3 16.8 %all_to_all.20 = bf16[8,2,8,4096]{3,2,1,0:T(8,128)(2,1)S(1)} all-to-all(bf16[8,2,8,4096]{3,2,1,0:T(8,128)(2,1)S(1)} %copy.65), channel_id=1, replica_groups=mesh['dp'=4,'section'=4,'expert'=8] {'expert'}, dimensions={0} | all-to-all | bytes 2097152 | tf_op jit(solution)/shard_map/all_to_all | solution.py:100
  105.1 1.9 stack.3
  107.0 0.0 copy-start.4
  107.0 194.1 %all_to_all.21 = bf16[16,128,4096]{2,1,0:T(8,128)(2,1)S(1)} all-to-all(bf16[16,128,4096]{2,1,0:T(8,128)(2,1)S(1)} %stack.3), channel_id=1, replica_groups=mesh['dp'=4,'section'=4,'expert'=8] {'dp','section'}, dimensions={0} | all-to-all | bytes 33554432 | tf_op jit(solution)/shard_map/all_to_all | solution.py:107
  301.1 5.7 %copy-done.2 = bf16[16,128,4096]{2,1,0:T(8,128)(2,1)} copy-done((bf16[16,128,4096]{2,1,0:T(8,128)(2,1)}, bf16[16,128,4096]{2,1,0:T(8,128)(2,1)S(1)}, u32[]{:S(2)}) %copy-start.2) | copy-done | bytes 16777240
  306.9 0.0 copy-done.4
  306.9 9.6 %fusion.5 = f32[2048,448]{0,1:T(8,128)} fusion(bf16[2048,4096]{1,0:T(8,128)(2,1)S(1)} %bitcast.111, bf16[1,448,4096]{2,1,0:T(8,128)(2,1)S(1)} %copy-done.4), kind=kOutput, calls=%fused_computation.11 | convolution fusion | flops 7516192768 | bytes 24117248 | tf_op jit(solution)/shard_map/dot_general | solution.py:112
  316.5 24.4 %convolution_convert_fusion = bf16[2048,4096]{1,0:T(8,128)(2,1)} fusion(bf16[1,448,4096]{2,1,0:T(8,128)(2,1)} %param.18, f32[2048,448]{0,1:T(8,128)} %fusion.5, bf16[2048,4096]{1,0:T(8,128)(2,1)} %bitcast.112, bf16[1,448,4096]{2,1,0:T(8,128)(2,1)} %param.17), kind=kOutput, calls=%fused_computation | convolution fusion | flops 15046279168 | bytes 44564480 | tf_op jit(solution)/shard_map/dot_general | solution.py:116
  340.8 0.0 reduce-scatter.5.cloned.1.call-update
  340.9 3.4 convolution_convert_fusion.2
  344.3 1.5 copy.108
  345.8 5.8 %all-to-all-start.3 = ((bf16[16,256,256]{1,2,0:T(8,128)(2,1)}), bf16[16,256,256]{1,2,0:T(8,128)(2,1)}, u32[]{:S(2)}, u32[]{:S(2)}) async-start(bf16[16,256,256]{1,2,0:T(8,128)(2,1)} %bitcast.110), calls=%async_computation.4 | async-start | bytes 4194304 | tf_op jit(solution)/shard_map/all_to_all | solution.py:20
  351.6 133.9 %reduce-scatter.5.cloned.1.call-done = bf16[128,4096]{1,0:T(8,128)(2,1)} async-done(((bf16[2048,4096]{1,0:T(8,128)(2,1)}), bf16[128,4096]{1,0:T(8,128)(2,1)}) %reduce-scatter.5.cloned.1.call-update) | async-done | bytes 1048592 | tf_op jit(solution)/shard_map/reduce_scatter | solution.py:115
  485.5 3.3 copy.66
  488.8 0.0 all-to-all-done.3
  488.8 4.2 all-to-all-start.2
  493.1 0.0 copy-start.1
  493.1 2.0 convert_reduce_fusion
  495.1 0.8 copy.73
  496.0 11.3 %all-to-all-done.2 = bf16[8,2,8,4096]{3,1,2,0:T(2,128)(2,1)} async-done(((bf16[8,2,8,4096]{3,1,2,0:T(2,128)(2,1)}), bf16[8,2,8,4096]{3,1,2,0:T(2,128)(2,1)}, u32[]{:S(2)}, u32[]{:S(2)}) %all-to-all-start.2) | async-done | bytes 1048608 | tf_op jit(solution)/shard_map/all_to_all | solution.py:121
  507.3 0.0 copy-done.3
  507.3 3.7 multiply_reduce_fusion
  511.0 1.1 copy.71
  512.1 0.7 copy.72
  512.8 0.0 copy-done.1
  (6 shorter events, 0.0 us)
Async XLA Ops:
  7.2 18.0 %copy-start = (bf16[256,4096]{1,0:T(8,128)(2,1)S(1)}, bf16[256,4096]{1,0:T(8,128)(2,1)}, u32[]{:S(2)}) copy-start(bf16[256,4096]{1,0:T(8,128)(2,1)} %param.15) | copy-start | bytes 6291460
  7.2 78.2 %reduce-scatter.7.cloned.1.call-start = ((), (), s32[]{:S(2)}) async-start(), calls=%async_computation.7 | async-start | bytes 4718592
  7.3 5.0 copy-start.5
  28.6 0.7 copy-start.6
  28.6 456.9 %reduce-scatter.5.cloned.1.call-start = ((), (), s32[]{:S(2)}) async-start(), calls=%async_computation.6 | async-start | bytes 17825792 | tf_op jit(solution)/shard_map/reduce_scatter | solution.py:115
  107.0 199.9 %copy-start.4 = (bf16[1,448,4096]{2,1,0:T(8,128)(2,1)S(1)}, bf16[1,448,4096]{2,1,0:T(8,128)(2,1)}, u32[]{:S(2)}) copy-start(bf16[1,448,4096]{2,1,0:T(8,128)(2,1)} %param.16) | copy-start | bytes 11010052
  301.1 5.7 %copy-start.2 = (bf16[16,128,4096]{2,1,0:T(8,128)(2,1)}, bf16[16,128,4096]{2,1,0:T(8,128)(2,1)S(1)}, u32[]{:S(2)}) copy-start(bf16[16,128,4096]{2,1,0:T(8,128)(2,1)S(1)} %all_to_all.21) | copy-start | bytes 50331652
  345.8 143.0 %all-to-all-start.3 = ((bf16[16,256,256]{1,2,0:T(8,128)(2,1)}), bf16[16,256,256]{1,2,0:T(8,128)(2,1)}, u32[]{:S(2)}, u32[]{:S(2)}) async-start(bf16[16,256,256]{1,2,0:T(8,128)(2,1)} %bitcast.110), calls=%async_computation.4 | async-start | bytes 4194304 | tf_op jit(solution)/shard_map/all_to_all | solution.py:20
  351.6 155.7 %copy-start.3 = (bf16[8,32768]{1,0:T(8,128)(2,1)S(1)}, bf16[8,32768]{1,0:T(8,128)(2,1)}, u32[]{:S(2)}) copy-start(bf16[8,32768]{1,0:T(8,128)(2,1)} %reduce-scatter.7.cloned.1.call-done) | copy-start | bytes 1572868
  488.8 18.5 %all-to-all-start.2 = ((bf16[8,2,8,4096]{3,1,2,0:T(2,128)(2,1)}), bf16[8,2,8,4096]{3,1,2,0:T(2,128)(2,1)}, u32[]{:S(2)}, u32[]{:S(2)}) async-start(bf16[8,2,8,4096]{3,1,2,0:T(2,128)(2,1)} %copy.66), calls=%async_computation.3 | async-start | bytes 2097152 | tf_op jit(solution)/shard_map/all_to_all | solution.py:121
  493.1 19.7 %copy-start.1 = (bf16[256,4096]{1,0:T(8,128)(2,1)S(1)}, bf16[256,4096]{1,0:T(8,128)(2,1)}, u32[]{:S(2)}) copy-start(bf16[256,4096]{1,0:T(8,128)(2,1)} %param.15) | copy-start | bytes 6291460
Sparse Core Ops, SparseCore 0:
  28.7 56.5 reduce-scatter.6
  341.0 144.4 reduce-scatter.4
